TPU v7x, 256 devices: a whole 4x4x8 slice. The times are simulated.
256 devices in a mesh: seq: 32 (over z_lo, y, core), kv: 8 (over x, z_hi).
Axes of the slice: x: 4, y: 4, z: 8 (z_hi: 2, z_lo: 4; z = z_hi * 4 + z_lo), core: 2. Of those that a mesh axis runs over, the one named last changes fastest.
Arguments:
- queries: bfloat16 [16384, 4096], P('seq', 'kv'), may hold values from -20 to 20
- key_rows: bfloat16 [16384, 1024], P('seq', 'kv'), may hold values from -6 to 6
- value_rows: bfloat16 [16384, 1024], P('seq', 'kv'), may hold values from -6 to 6
- out_weight: bfloat16 [4096, 4096], P('kv', 'seq'), may hold values from -0.1875 to 0.1875
- vertical: int32 [32, 16], replicated, may hold values from 0 to 126, all different within a row
- slash_offsets: int32 [32, 16], replicated, may hold values from 0 to 510
Outputs:
- projected: bfloat16 [16384, 4096], P('seq', 'kv')
Inputs may be any that keep to these rules, and one draw needn't show every extreme that they name: `vertical`: each row lists distinct entries.
All inputs are finite; a program needn't handle non-finite values.
Results may differ from a plain program's by a relative error of at most 0.015.
Values may be sent and summed in bfloat16 or wider, within the bound.
A program may use at most 128 MiB of HBM per device.

v0:
```python
import math

import jax
import jax.numpy as jnp
from jax import lax
from jax.sharding import PartitionSpec as P

HEAD_DIM = 128
BLOCK = 128


def from_behind(array, axis, by):
    peers = lax.axis_size(axis)
    pairs = [(i, i + by) for i in range(peers) if 0 <= i + by < peers]
    return lax.ppermute(array, axis, pairs)


def attend(
    query_head, window_key, window_value, picked_key, picked_value, offsets, column_ids, first_row
):
    length = query_head.shape[0]
    factor = 1.0 / math.sqrt(query_head.shape[1])
    window_scores = jnp.dot(query_head, window_key.T, preferred_element_type=jnp.float32) * factor
    picked_scores = jnp.dot(query_head, picked_key.T, preferred_element_type=jnp.float32) * factor
    query_pos = first_row + jnp.arange(length, dtype=jnp.int32)
    key_pos = first_row - length + jnp.arange(2 * length, dtype=jnp.int32)
    distance = query_pos[:, None] - key_pos[None, :]
    on_slash = (distance == 0) | jnp.any(
        distance[:, :, None] == (offsets + 1)[None, None, :], axis=-1
    )
    on_column = jnp.any((key_pos // BLOCK)[:, None] == column_ids[None, :], axis=-1)
    earlier_column = on_column & (key_pos < first_row)
    window_mask = (
        (key_pos >= 0)[None, :]
        & (distance >= 0)
        & (on_slash | on_column[None, :])
        & (~earlier_column)[None, :]
    )
    keep_block = column_ids < first_row // BLOCK
    picked_mask = jnp.repeat(keep_block, BLOCK)[None, :]
    window_scores = jnp.where(window_mask, window_scores, -jnp.inf)
    picked_scores = jnp.where(picked_mask, picked_scores, -jnp.inf)
    row_peak = jnp.maximum(jnp.max(window_scores, axis=1), jnp.max(picked_scores, axis=1))[:, None]
    window_prob = jnp.exp(window_scores - row_peak)
    picked_prob = jnp.exp(picked_scores - row_peak)
    denominator = jnp.sum(window_prob, axis=1) + jnp.sum(picked_prob, axis=1)
    mixed = jnp.dot(
        window_prob.astype(jnp.bfloat16), window_value, preferred_element_type=jnp.float32
    )
    mixed = mixed + jnp.dot(
        picked_prob.astype(jnp.bfloat16), picked_value, preferred_element_type=jnp.float32
    )
    return mixed / denominator[:, None]


def shards(queries, key_rows, value_rows, out_weight, vertical, slash_offsets):
    length = queries.shape[0]
    group_heads = queries.shape[1] // HEAD_DIM
    shard_index = lax.axis_index("seq")
    group_index = lax.axis_index("kv")
    first_row = shard_index * length
    column_all = jnp.concatenate(
        [jnp.zeros((vertical.shape[0], 1), jnp.int32), vertical + 1], axis=1
    )
    column_ids = lax.dynamic_slice_in_dim(column_all, group_index * group_heads, group_heads, 0)
    offsets_here = lax.dynamic_slice_in_dim(
        slash_offsets, group_index * group_heads, group_heads, 0
    )
    stacked = jnp.stack([key_rows, value_rows])
    previous = from_behind(stacked, "seq", 1)
    window = jnp.concatenate([previous, stacked], axis=1)
    gathered = lax.all_gather(stacked, "seq", axis=1, tiled=True)
    picked = gathered.reshape(2, -1, BLOCK, HEAD_DIM)[:, column_ids]
    picked = picked.reshape(2, group_heads, -1, HEAD_DIM)
    outputs = []
    for member in range(group_heads):
        query_head = queries[:, member * HEAD_DIM : (member + 1) * HEAD_DIM]
        outputs.append(
            attend(
                query_head,
                window[0],
                window[1],
                picked[0, member],
                picked[1, member],
                offsets_here[member],
                column_ids[member],
                first_row,
            )
        )
    attention = jnp.concatenate(outputs, axis=1).astype(jnp.bfloat16)
    partials = jnp.dot(
        attention,
        lax.all_gather(out_weight, "seq", axis=1, tiled=True),
        preferred_element_type=jnp.float32,
    )
    return lax.psum_scatter(partials.astype(jnp.bfloat16), "kv", scatter_dimension=1, tiled=True)


def solution(mesh):
    in_specs = (P("seq", "kv"), P("seq", "kv"), P("seq", "kv"), P("kv", "seq"), P(), P())
    out_specs = P("seq", "kv")
    return jax.shard_map(shards, mesh=mesh, in_specs=in_specs, out_specs=out_specs, check_vma=False)
```

profile of v0, /device:TPU:8, one launch (start us, length us, event | category | flops | bytes accessed | tf_op | source)
XLA Modules:
  0.0 293.1 jit_solution(18306173549735968469)
XLA Ops:
  6.5 1.7 pad_maximum_fusion
  8.3 1.9 collective-permute-start
  10.4 0.7 broadcast_add_fusion
  11.2 0.2 fusion.63
  11.5 0.1 copy.16
  11.6 0.1 reshape.168
  11.7 1.1 fusion.70
  12.7 1.6 broadcast_subtract_fusion
  14.3 1.9 copy.14
  16.3 0.1 compare_reduce_fusion.7
  16.6 40.8 %compare_reduce_fusion.3 = (pred[512,1024]{1,0:T(8,128)(4,1)S(1)}, pred[512,1024]{1,0:T(8,128)(4,1)S(1)}, pred[512,1024]{1,0:T(8,128)(4,1)S(1)}, pred[512,1024]{1,0:T(8,128)(4,1)S(1)}) fusion(s32[512,1024]{1,0:T(8,128)S(1)} %copy.14, s32[16]{0:T(128)S(1)} %get-tuple-element.9, s32[16]{0:T(128)S(1)} %get-tuple-element.11, s32[16]{0:T(128)S(1)} %get-tuple-element.10, ...), kind=kLoop, calls=%fused_computation.4 | loop fusion | flops 65011712 | bytes 4194560 | tf_op jit(solution)/shard_map/reduce_or | solution.py:28
  57.5 0.6 copy.15
  58.1 0.6 copy.18
  58.8 0.6 copy.19
  59.4 0.6 copy.20
  60.1 3.0 %fusion.91 = (f32[512]{0:T(512)S(1)}, f32[512,1024]{0,1:T(8,128)}) fusion(bf16[512,512]{1,0:T(8,128)(2,1)S(1)} %copy-done.3, bf16[2,1024,128]{2,1,0:T(8,128)(2,1)S(1)} %maximum_maximum_fusion, pred[1024]{0:T(1024)(128)(4,1)S(1)} %get-tuple-element.41, pred[1024]{0:T(1024)(128)(4,1)S(1)} %get-tuple-element.17, pred[512,1024]{0,1:T(32,128)(4,1)S(1)} %copy.15, ...), kind=kOutput, calls=%fused_computation.155 | convolution fusion | flops 139984384 | bytes 3025920 | tf_op jit(solution)/shard_map/dot_general | solution.py:23
  63.1 2.9 fusion.89
  66.0 2.9 fusion.87
  68.9 1.2 fusion.85
  70.1 11.1 %all-gather.3.cloned.1.call-done = bf16[2,16384,128]{2,1,0:T(8,128)(2,1)} async-done(((bf16[2,512,128]{2,1,0:T(8,128)(2,1)}), bf16[2,16384,128]{2,1,0:T(8,128)(2,1)}) %all-gather.3.cloned.1.call-update) | async-done | bytes 8388624 | tf_op jit(solution)/shard_map/all_gather | solution.py:72
  81.1 8.8 %gather_fusion = bf16[68,2,128,128]{3,2,1,0:T(8,128)(2,1)} fusion(bf16[2,128,128,128]{3,2,1,0:T(8,128)(2,1)} %bitcast.85, s32[1024]{0:T(1024)S(1)} %pad_clamp_fusion), kind=kCustom, calls=%fused_computation | custom fusion | bytes 8913168 | tf_op jit(solution)/shard_map/gather | solution.py:73
  89.9 3.2 %copy.17 = bf16[4,17,2,128,128]{4,3,1,0,2:T(8,128)(2,1)S(1)} copy(bf16[4,17,2,128,128]{4,3,2,1,0:T(8,128)(2,1)} %bitcast.84) | data formatting | bytes 8912896 | tf_op jit(solution)/shard_map/gather | solution.py:73
  93.1 0.8 fusion.92
  93.9 0.9 copy-done.1
  94.7 0.4 fusion.24
  95.1 0.7 fusion.4
  95.8 0.8 fusion.90
  96.6 0.1 copy-done.2
  96.7 0.4 fusion.26
  97.1 0.7 fusion.6
  97.7 0.8 fusion.88
  98.5 0.2 copy-done
  98.7 0.4 fusion.28
  99.0 0.7 fusion.8
  99.7 0.8 fusion.86
  100.5 0.4 fusion.30
  100.9 0.7 fusion.10
  101.5 0.8 fusion.18
  102.3 0.5 fusion.36
  102.8 0.8 fusion.16
  103.6 0.5 fusion.37
  104.1 0.8 fusion.14
  104.9 0.5 fusion.38
  105.3 0.8 fusion.12
  106.1 0.7 fusion.39
  106.8 46.2 %all-gather.5.cloned.1.call-done = bf16[512,4096]{1,0:T(8,128)(2,1)} async-done(((bf16[512,128]{1,0:T(8,128)(2,1)}), bf16[512,4096]{1,0:T(8,128)(2,1)}) %all-gather.5.cloned.1.call-update) | async-done | bytes 4194320 | tf_op jit(solution)/shard_map/all_gather | solution.py:93
  153.0 6.5 %convolution_convert_fusion = bf16[512,4096]{1,0:T(8,128)(2,1)} fusion(bf16[512,4096]{1,0:T(8,128)(2,1)} %all-gather.5.cloned.1.call-done, bf16[512,128]{0,1:T(8,128)(2,1)S(1)} %fusion.39, bf16[512,128]{0,1:T(8,128)(2,1)S(1)} %fusion.38, bf16[512,128]{0,1:T(8,128)(2,1)S(1)} %fusion.37, bf16[512,128]{0,1:T(8,128)(2,1)S(1)} %fusion.36), kind=kOutput, calls=%fused_computation.5 | convolution fusion | flops 2151677952 | bytes 8912896 | tf_op jit(solution)/shard_map/dot_general | solution.py:91
  159.5 127.1 %reduce-scatter.2.cloned.1.call-done = bf16[512,512]{1,0:T(8,128)(2,1)} async-done(((bf16[512,4096]{1,0:T(8,128)(2,1)}), bf16[512,512]{1,0:T(8,128)(2,1)}) %reduce-scatter.2.cloned.1.call-update) | async-done | bytes 524304 | tf_op jit(solution)/shard_map/reduce_scatter | solution.py:96
  (39 shorter events, 0.7 us)
Async XLA Ops:
  6.5 74.6 %all-gather.3.cloned.1.call-start = ((), (), s32[]{:S(2)}) async-start(), calls=%async_computation.1 | async-start | bytes 8650752 | tf_op jit(solution)/shard_map/all_gather | solution.py:72
  8.3 144.7 %all-gather.5.cloned.1.call-start = ((), (), s32[]{:S(2)}) async-start(), calls=%async_computation.2 | async-start | bytes 4325376 | tf_op jit(solution)/shard_map/all_gather | solution.py:93
  8.3 51.7 %collective-permute-start = (bf16[2,512,128]{2,1,0:T(8,128)(2,1)}, bf16[2,512,128]{2,1,0:T(8,128)(2,1)S(1)}, u32[]{:S(2)}, u32[]{:S(2)}) collective-permute-start(bf16[2,512,128]{2,1,0:T(8,128)(2,1)} %pad_maximum_fusion), channel_id=1, source_target_pairs={{0,8},{8,16},{16,24},{24,32},{32,40},{40,48},{48,56},{56,64},{64,7... | collective-permute-start | bytes 786440 | tf_op jit(solution)/shard_map/ppermute | solution.py:15
  10.3 276.4 %reduce-scatter.2.cloned.1.call-start = ((), (), s32[]{:S(2)}) async-start(), calls=%async_computation.3 | async-start | bytes 4718592 | tf_op jit(solution)/shard_map/reduce_scatter | solution.py:96
  16.6 43.5 %copy-start.4 = (bf16[512,128]{1,0:T(8,128)(2,1)S(1)}, bf16[512,128]{1,0:T(8,128)(2,1)}, u32[]{:S(2)}) copy-start(bf16[512,128]{1,0:T(8,128)(2,1)} %param.8) | copy-start | bytes 393220
  16.6 43.5 %copy-start.5 = (bf16[512,128]{1,0:T(8,128)(2,1)S(1)}, bf16[512,128]{1,0:T(8,128)(2,1)}, u32[]{:S(2)}) copy-start(bf16[512,128]{1,0:T(8,128)(2,1)} %param.7) | copy-start | bytes 393220
  16.6 43.5 %copy-start.3 = (bf16[512,512]{1,0:T(8,128)(2,1)S(1)}, bf16[512,512]{1,0:T(8,128)(2,1)}, u32[]{:S(2)}) copy-start(bf16[512,512]{1,0:T(8,128)(2,1)} %param.6) | copy-start | bytes 1572868
  93.1 1.7 copy-start.1
  95.1 1.6 copy-start.2
  97.1 1.6 copy-start
Sparse Core Ops, SparseCore 0:
  9.2 71.8 all-gather.2
  82.9 70.0 all-gather.4
  159.6 126.9 reduce-scatter.1
where the time goes:
time: 294 us; the launch traced here: 293 us
  waiting for transfers between devices  184 us (63%)
  other arithmetic  50.4 us (17%)
  matrix products  24.7 us (8%)
  local copies, waits for them, and re-layouts  18.2 us (6%)
  between operations  13.4 us (5%)
    reduce_scatter x1, waiting for transfers between devices, shards(): lax.psum_scatter(partials.astype(jnp.bfloat16), 'kv', scatter_dimension=1...  127 us
    all_gather x1, waiting for transfers between devices, shards(): lax.all_gather(out_weight, 'seq', axis=1, tiled=True)  46.2 us
    reduce_or x1, other arithmetic, attend(): jnp.any(distance[:, :, None] == (offsets + 1)[None, None, :], axis=-1)  40.8 us
    gather x2, local copies, waits for them, and re-layouts, shards(): picked = gathered.reshape(2, -1, BLOCK, HEAD_DIM)[:, column_ids]  11.9 us
    all_gather x1, waiting for transfers between devices, shards(): gathered = lax.all_gather(stacked, 'seq', axis=1, tiled=True)  11.1 us
    dot_general x4, matrix products, attend(): jnp.dot(query_head, window_key.T, preferred_element_type=jnp.float32)  9.96 us
    dot_general x1, matrix products, shards(): jnp.dot(attention, lax.all_gather(out_weight, 'seq', axis=1, tiled=True),...  6.48 us
  transfers between devices with their start and end apart: 4, of which 3 were waited for; matrix products, arithmetic and copies ran while one was open for 29% of the time, Pallas kernels for 0%

commit v1 on v0

v1 whole, which is shorter than its diff:
```python
import functools
import math

import jax
import jax.numpy as jnp
from jax import lax
from jax.experimental import pallas as pl
from jax.experimental.pallas import tpu as pltpu
from jax.sharding import PartitionSpec as P

MESH = pl.DeviceIdType.MESH
HEAD_DIM = 128
BLOCK = 128
GROUP = 4
ROWS = 512
NV = 16
NS = 16
NPICK = NV + 1
RBLK = ROWS // BLOCK
WIN = 5 * BLOCK
PICK = NPICK * BLOCK
NEG = -1e30
SCALE = math.log2(math.e) / math.sqrt(HEAD_DIM)


def dot(a, b):
    return jnp.dot(a, b, preferred_element_type=jnp.float32)


def dot_t(a, b):
    return lax.dot_general(a, b, (((1,), (1,)), ((), ())), preferred_element_type=jnp.float32)


def kernel(
    vert, slash, q_ref, k_hbm, v_hbm, w_hbm, out_ref,
    kvbuf, wbuf, abuf, kcat, vcat, sbias, own, zsrc, relay, zdst,
    lsem, zs, zr, ys, yr, ys2, yr2, cs, cr,
    wxs, wxr, wzs, wzr, wys, wyr, wys2, wyr2, wcs, wcr,
    xs, xr, xs2, xr2, es, er, fs, fr,
):
    seq = lax.axis_index("seq")
    kv = lax.axis_index("kv")
    core = seq % 2
    y = (seq // 2) % 4
    p = seq // 8
    x = kv // 2
    zh = kv % 2
    z = zh * 4 + p

    def dev(x_, y_, z_, c_):
        return (((z_ % 4) * 4 + y_) * 2 + c_, x_ * 2 + z_ // 4)

    sib = dev(x, y, z, 1 - core)
    y_to = [dev(x, (y + 1) % 4, z, core), dev(x, (y + 3) % 4, z, core)]
    z_up = dev(x, y, (z + 1) % 8, core)
    z_dn = dev(x, y, (z + 7) % 8, core)
    z_two = [dev(x, y, (z + 2) % 8, core), dev(x, y, (z + 6) % 8, core)]
    x_to = [dev((x + 1) % 4, y, z, core), dev((x + 3) % 4, y, z, core)]
    x_far = dev((x + 2) % 4, y, z, core)

    def rc(src, dst, ss, rs, d):
        return pltpu.make_async_remote_copy(
            src_ref=src, dst_ref=dst, send_sem=ss, recv_sem=rs, device_id=d, device_id_type=MESH
        )

    def chunk(q, yy, c):
        return kvbuf.at[pl.ds(4 + 4 * ((q * 4 + yy) * 2 + c), 4)]

    def half(q, yy, c, h):
        return kvbuf.at[pl.ds(4 + 4 * ((q * 4 + yy) * 2 + c) + 2 * h, 2)]

    base = 4 + 4 * seq
    copies = [
        pltpu.make_async_copy(k_hbm, kvbuf.at[pl.ds(base, 4), 0], lsem.at[0]),
        pltpu.make_async_copy(v_hbm, kvbuf.at[pl.ds(base, 4), 1], lsem.at[1]),
    ]
    for c in copies:
        c.start()
    w_local = pltpu.make_async_copy(w_hbm, wbuf.at[y, core, x], lsem.at[2])

    @pl.when(x == p)
    def _():
        w_local.start()

    barrier = pltpu.get_barrier_semaphore()
    partners = [sib, *y_to, z_up, z_dn, *z_two, *x_to, x_far]
    for d in partners:
        pl.semaphore_signal(barrier, inc=1, device_id=d, device_id_type=MESH)
    for c in copies:
        c.wait()
    pl.semaphore_wait(barrier, len(partners))

    def z_send(t):
        return rc(chunk(p - t, y, core), chunk(p - t, y, core), zs.at[t], zr.at[t + 1], z_up)

    def y_send(t, d):
        return rc(chunk(p - t, y, core), chunk(p - t, y, core), ys.at[d, t], yr.at[d, t], y_to[d])

    def y_got(t, d):
        c = chunk(p - t, (y + 3 - 2 * d) % 4, core)
        return rc(c, c, ys.at[d, t], yr.at[d, t], y_to[d])

    def y_next(t, d):
        c = half(p - t, (y + 3 - 2 * d) % 4, core, d)
        return rc(c, c, ys2.at[d, t], yr2.at[d, t], y_to[d])

    def y_far(t, d):
        c = half(p - t, (y + 2) % 4, core, d)
        return rc(c, c, ys2.at[d, t], yr2.at[d, t], y_to[d])

    def c_send(t, off):
        c = chunk(p - t, (y + off) % 4, core)
        return rc(c, c, cs.at[t, off], cr.at[t, off], sib)

    def c_got(t, off):
        c = chunk(p - t, (y + off) % 4, 1 - core)
        return rc(c, c, cs.at[t, off], cr.at[t, off], sib)

    def enter(t):
        @pl.when(p >= t)
        def _():
            if t > 0:
                c = chunk(p - t, y, core)
                rc(c, c, zs.at[t], zr.at[t], z_up).wait_recv()
            if t < 3:
                @pl.when(p < 3)
                def _():
                    z_send(t).start()
            for d in range(2):
                y_send(t, d).start()
            c_send(t, 0).start()

    def onward(t):
        @pl.when(p >= t)
        def _():
            for d in range(2):
                y_got(t, d).wait_recv()
                y_next(t, d).start()
                c_send(t, 3 - 2 * d).start()

    def finish(t):
        @pl.when(p >= t)
        def _():
            for d in range(2):
                y_far(t, d).wait_recv()
            c_send(t, 2).start()

    def w_move():
        return rc(w_hbm, wbuf.at[y, core, x], wxs.at[0], wxr.at[x], dev(p, y, z, core))

    def wz_send(i, d):
        c = wbuf.at[y, core, i]
        return rc(c, c, wzs.at[d, i], wzr.at[i], z_up if d == 0 else z_dn)

    def w_pass(i):
        c = wbuf.at[y, core, i]

        @pl.when((x == p) & (x != i))
        def _():
            rc(c, c, wxs.at[0], wxr.at[i], sib).wait_recv()

        @pl.when(x != p)
        def _():
            rc(c, c, wzs.at[0, i], wzr.at[i], sib).wait_recv()

        @pl.when((p >= x) & (p < 3))
        def _():
            wz_send(i, 0).start()

        @pl.when((p <= x) & (p > 0))
        def _():
            wz_send(i, 1).start()

    def wy(yy, d, ss, rs):
        c = wbuf.at[yy, core]
        return rc(c, c, ss, rs, y_to[d])

    def wy_half(yy, d):
        c = wbuf.at[yy, core, pl.ds(2 * d, 2)]
        return rc(c, c, wys2.at[d], wyr2.at[d], y_to[d])

    def wc(off, c_):
        c = wbuf.at[(y + off) % 4, c_]
        return rc(c, c, wcs.at[off], wcr.at[off], sib)

    @pl.when(x != p)
    def _():
        w_move().start()

    enter(0)

    kvbuf[0:4] = jnp.zeros((4, 2, BLOCK, HEAD_DIM), jnp.bfloat16)

    def mask_step(n, carry):
        m, strip = n // 4, n % 4
        i = lax.broadcasted_iota(jnp.int32, (32, WIN), 0) + strip * 32
        j = lax.broadcasted_iota(jnp.int32, (32, WIN), 1)
        d = 4 * BLOCK + i - j
        b = jnp.where(d == 0, 0.0, NEG)
        for e in range(NS):
            b = jnp.where(d == slash[kv * GROUP + m, e] + 1, 0.0, b)
        sbias[m, pl.ds(pl.multiple_of(strip * 32, 32), 32), :] = b
        return carry

    lax.fori_loop(0, 16, mask_step, 0)

    enter(1)
    onward(0)
    enter(2)
    onward(1)
    finish(0)
    enter(3)
    onward(2)
    finish(1)

    @pl.when(x == p)
    def _():
        w_local.wait()

    for i in range(4):
        w_pass(i)
    onward(3)
    finish(2)
    finish(3)
    for t in range(4):
        @pl.when(p >= t)
        def _(t=t):
            for off in range(4):
                c_got(t, off).wait_recv()

    for d in range(2):
        wy(y, d, wys.at[d], wyr.at[d]).start()
    wc(0, core).start()

    def gather(m, carry):
        for j in range(NPICK):
            b = 0 if j == 0 else vert[kv * GROUP + m, j - 1] + 1
            at = 4 + (0 if j == 0 else jnp.where(b < 4 * seq + 4, b, 0))
            kcat[m, j * BLOCK : (j + 1) * BLOCK, :] = kvbuf[at, 0]
            vcat[m, j * BLOCK : (j + 1) * BLOCK, :] = kvbuf[at, 1]
        return carry

    lax.fori_loop(0, GROUP, gather, 0)

    wi = lax.broadcasted_iota(jnp.int32, (BLOCK, WIN), 0)
    wj = lax.broadcasted_iota(jnp.int32, (BLOCK, WIN), 1)
    lane = lax.broadcasted_iota(jnp.int32, (1, WIN), 1)

    def attend(r):
        rows = pl.ds(pl.multiple_of(r * BLOCK, BLOCK), BLOCK)
        here = 4 * seq + r
        for m in range(GROUP):
            cols = slice(m * HEAD_DIM, (m + 1) * HEAD_DIM)
            q = q_ref[rows, cols]
            kw = kvbuf[pl.ds(here, 5), 0].reshape(WIN, HEAD_DIM)
            vw = kvbuf[pl.ds(here, 5), 1].reshape(WIN, HEAD_DIM)
            bcol = here - 4 + lane // BLOCK
            oncol = bcol <= 0
            pb = [jnp.full((1, BLOCK), jnp.where(here > 0, 0.0, NEG), jnp.float32)]
            for e in range(NV):
                b = vert[kv * GROUP + m, e] + 1
                oncol = oncol | (bcol == b)
                pb.append(jnp.full((1, BLOCK), jnp.where(b < here, 0.0, NEG), jnp.float32))
            alt = jnp.where((wj >= 4 * BLOCK) & (wi >= wj - 4 * BLOCK), 0.0, NEG)
            bias = jnp.where(oncol, alt, sbias[m])
            sw = dot_t(q, kw) + bias
            sp = dot_t(q, kcat[m]) + jnp.concatenate(pb, axis=1)
            peak = jnp.maximum(
                jnp.max(sw, axis=1, keepdims=True), jnp.max(sp, axis=1, keepdims=True)
            )
            pw = jnp.exp2((sw - peak) * SCALE).astype(jnp.bfloat16)
            pp = jnp.exp2((sp - peak) * SCALE).astype(jnp.bfloat16)
            ones_w = jnp.ones((WIN, HEAD_DIM), jnp.bfloat16)
            ones_p = jnp.ones((PICK, HEAD_DIM), jnp.bfloat16)
            o = dot(pw, jnp.concatenate([vw, ones_w], axis=1))
            o = o + dot(pp, jnp.concatenate([vcat[m], ones_p], axis=1))
            abuf[x, rows, cols] = (o[:, :HEAD_DIM] / o[:, HEAD_DIM:]).astype(jnp.bfloat16)

    def a_part(xx, r):
        return abuf.at[xx, pl.ds(pl.multiple_of(r * BLOCK, BLOCK), BLOCK)]

    def a_half(xx, r, d):
        return abuf.at[xx, pl.ds(pl.multiple_of(r * BLOCK + d * 64, 64), 64)]

    def x_send(r, d):
        return rc(a_part(x, r), a_part(x, r), xs.at[d, r], xr.at[d, r], x_to[d])

    def x_got(r, d):
        c = a_part((x + 3 - 2 * d) % 4, r)
        return rc(c, c, xs.at[d, r], xr.at[d, r], x_to[d])

    def x_next(r, d):
        c = a_half((x + 3 - 2 * d) % 4, r, d)
        return rc(c, c, xs2.at[d, r], xr2.at[d, r], x_to[d])

    def x_last(r, d):
        c = a_half((x + 2) % 4, r, d)
        return rc(c, c, xs2.at[d, r], xr2.at[d, r], x_to[d])

    def e_send(r, d):
        src = zsrc.at[r, pl.ds(d * 64, 64)]
        return rc(src, relay.at[r, d], es.at[d, r], er.at[d, r], z_two[d])

    def f_send(r, d):
        return rc(relay.at[r, d], zdst.at[r, pl.ds(d * 64, 64)], fs.at[d, r], fr.at[d, r], z_two[d])

    def product(r, h):
        rows = pl.ds(pl.multiple_of(r * BLOCK, BLOCK), BLOCK)
        acc = None
        for i in range(4):
            w = jnp.concatenate(
                [wbuf[2 * h + n // 2, n % 2, i] for n in range(4)], axis=1
            )
            part = dot(abuf[i, rows, :], w)
            acc = part if acc is None else acc + part
        return acc

    def step(it, carry):
        @pl.when(it < 4)
        def _():
            attend(it)
            for d in range(2):
                x_send(it, d).start()

        @pl.when(it == 1)
        def _():
            for d in range(2):
                yy = (y + 3 - 2 * d) % 4
                wy(yy, d, wys.at[d], wyr.at[d]).wait_recv()
                wy_half(yy, d).start()
                wc(3 - 2 * d, core).start()

        @pl.when(it == 2)
        def _():
            for d in range(2):
                wy_half((y + 2) % 4, d).wait_recv()
            wc(2, core).start()
            for off in range(4):
                wc(off, 1 - core).wait_recv()

        @pl.when((it >= 1) & (it < 5))
        def _():
            for d in range(2):
                x_got(it - 1, d).wait_recv()
                x_next(it - 1, d).start()

        @pl.when((it >= 2) & (it < 6))
        def _():
            r = it - 2
            for d in range(2):
                x_last(r, d).wait_recv()
            zsrc[r] = product(r, 1 - zh).astype(jnp.bfloat16)
            for d in range(2):
                e_send(r, d).start()
            own[r] = product(r, zh)

        @pl.when((it >= 3) & (it < 7))
        def _():
            for d in range(2):
                e_send(it - 3, d).wait_recv()
                f_send(it - 3, d).start()

        @pl.when(it >= 4)
        def _():
            r = it - 4
            for d in range(2):
                f_send(r, d).wait_recv()
            rows = pl.ds(pl.multiple_of(r * BLOCK, BLOCK), BLOCK)
            out_ref[rows, :] = (own[r] + zdst[r].astype(jnp.float32)).astype(jnp.bfloat16)

        return carry

    lax.fori_loop(0, 8, step, 0)

    for t in range(4):
        @pl.when(p >= t)
        def _(t=t):
            if t < 3:
                @pl.when(p < 3)
                def _():
                    z_send(t).wait_send()
            for d in range(2):
                y_send(t, d).wait_send()
                y_next(t, d).wait_send()
            for off in range(4):
                c_send(t, off).wait_send()

    @pl.when(x != p)
    def _():
        w_move().wait_send()

    for i in range(4):
        @pl.when((p >= x) & (p < 3))
        def _(i=i):
            wz_send(i, 0).wait_send()

        @pl.when((p <= x) & (p > 0))
        def _(i=i):
            wz_send(i, 1).wait_send()

    for d in range(2):
        wy(y, d, wys.at[d], wyr.at[d]).wait_send()
        wy_half((y + 3 - 2 * d) % 4, d).wait_send()
    for off in range(4):
        wc(off, core).wait_send()

    def drain(r, carry):
        for d in range(2):
            x_send(r, d).wait_send()
            x_next(r, d).wait_send()
            e_send(r, d).wait_send()
            f_send(r, d).wait_send()
        return carry

    lax.fori_loop(0, 4, drain, 0)


def shards(queries, key_rows, value_rows, out_weight, vertical, slash_offsets):
    bf16 = jnp.bfloat16
    dma = pltpu.SemaphoreType.DMA
    smem = pl.BlockSpec(memory_space=pltpu.SMEM)
    vmem = pl.BlockSpec(memory_space=pltpu.VMEM)
    anyspace = pl.BlockSpec(memory_space=pl.ANY)
    return pl.pallas_call(
        kernel,
        out_shape=jax.ShapeDtypeStruct((ROWS, ROWS), bf16),
        in_specs=[smem, smem, vmem, anyspace, anyspace, anyspace],
        out_specs=vmem,
        scratch_shapes=[
            pltpu.VMEM((132, 2, BLOCK, HEAD_DIM), bf16),
            pltpu.VMEM((4, 2, 4, ROWS, 128), bf16),
            pltpu.VMEM((4, ROWS, ROWS), bf16),
            pltpu.VMEM((GROUP, PICK, HEAD_DIM), bf16),
            pltpu.VMEM((GROUP, PICK, HEAD_DIM), bf16),
            pltpu.VMEM((GROUP, BLOCK, WIN), jnp.float32),
            pltpu.VMEM((RBLK, BLOCK, ROWS), jnp.float32),
            pltpu.VMEM((RBLK, BLOCK, ROWS), bf16),
            pltpu.VMEM((RBLK, 2, 64, ROWS), bf16),
            pltpu.VMEM((RBLK, BLOCK, ROWS), bf16),
            dma((3,)),
            dma((4,)), dma((4,)),
            dma((2, 4)), dma((2, 4)), dma((2, 4)), dma((2, 4)),
            dma((4, 4)), dma((4, 4)),
            dma((1,)), dma((4,)),
            dma((2, 4)), dma((4,)),
            dma((2,)), dma((2,)), dma((2,)), dma((2,)),
            dma((4,)), dma((4,)),
            dma((2, 4)), dma((2, 4)), dma((2, 4)), dma((2, 4)),
            dma((2, 4)), dma((2, 4)), dma((2, 4)), dma((2, 4)),
        ],
        compiler_params=pltpu.CompilerParams(
            collective_id=0, has_side_effects=True, vmem_limit_bytes=56 * 1024 * 1024
        ),
    )(
        vertical,
        slash_offsets,
        queries,
        key_rows.reshape(4, BLOCK, HEAD_DIM),
        value_rows.reshape(4, BLOCK, HEAD_DIM),
        out_weight,
    )


def solution(mesh):
    in_specs = (P("seq", "kv"), P("seq", "kv"), P("seq", "kv"), P("kv", "seq"), P(), P())
    out_specs = P("seq", "kv")
    return jax.shard_map(shards, mesh=mesh, in_specs=in_specs, out_specs=out_specs, check_vma=False)
```

time: 294 us -> 108 us (0.37)
  the two profiles are of different devices: /device:TPU:8 before, /device:TPU:13 now
where the time goes in v1:
time: 108 us
  Pallas kernels  104 us (96%)
  local copies, waits for them, and re-layouts  3.94 us (4%)
    pallas_call x1, Pallas kernels, shards(): pl.pallas_call(kernel, out_shape=jax.ShapeDtypeStruct((ROWS, ROWS), bf16)...  104 us
    unnamed x5, local copies, waits for them, and re-layouts  3.94 us

profile of v1, /device:TPU:13, one launch (start us, length us, event | category | flops | bytes accessed | tf_op | source)
XLA Modules:
  0.0 107.8 jit_solution(4817747369118829049)
XLA Ops:
  0.0 0.0 copy-start
  0.0 1.4 %copy.7.vert = s32[32,16]{1,0:T(8,128)} copy(s32[32,16]{0,1:T(8,128)} %param.10) | data formatting | bytes 4096 | tf_op args[4]
  1.4 0.0 copy-done
  1.4 0.7 copy.8.slash
  2.1 103.9 %shard_map.64 = bf16[512,512]{1,0:T(8,128)(2,1)} custom-call(s32[32,16]{1,0:T(8,128)} %copy.7.vert, s32[32,16]{1,0:T(8,128)} %copy.8.slash, bf16[512,512]{1,0:T(8,128)(2,1)} %q_ref.1, bf16[4,128,128]{2,1,0:T(8,128)(2,1)} %bitcast.2, bf16[4,128,128]{2,1,0:T(8,128)(2,1)} %bitcast.3, bf16[512,128]{1,0:T(8,128)(2,1)} %w_hbm.1), custom_call_target="tpu_custom_call" | custom-call | tf_op jit(solution)/shard_map/pallas_call | solution.py:424
  106.0 1.9 %copy.10 = bf16[512,512]{1,0:T(8,128)(2,1)} copy(bf16[512,512]{1,0:T(8,128)(2,1)} %shard_map.64) | data formatting | bytes 1048576
Async XLA Ops:
  0.0 1.4 %copy-start = (s32[32,16]{0,1:T(8,128)S(1)}, s32[32,16]{0,1:T(8,128)}, u32[]{:S(2)}) copy-start(s32[32,16]{0,1:T(8,128)} %param.11) | copy-start | bytes 6148

commit v2 on v1

--- a/solution.py
+++ b/solution.py
@@ -33,10 +33,10 @@
 
 def kernel(
     vert, slash, q_ref, k_hbm, v_hbm, w_hbm, out_ref,
-    kvbuf, wbuf, abuf, kcat, vcat, sbias, own, zsrc, relay, zdst,
+    kvbuf, wbuf, abuf, kcat, vcat, sbias, zsrc, zdst,
     lsem, zs, zr, ys, yr, ys2, yr2, cs, cr,
     wxs, wxr, wzs, wzr, wys, wyr, wys2, wyr2, wcs, wcr,
-    xs, xr, xs2, xr2, es, er, fs, fr,
+    xs, xr, xs2, xr2, es, er,
 ):
     seq = lax.axis_index("seq")
     kv = lax.axis_index("kv")
@@ -54,9 +54,8 @@
     y_to = [dev(x, (y + 1) % 4, z, core), dev(x, (y + 3) % 4, z, core)]
     z_up = dev(x, y, (z + 1) % 8, core)
     z_dn = dev(x, y, (z + 7) % 8, core)
-    z_two = [dev(x, y, (z + 2) % 8, core), dev(x, y, (z + 6) % 8, core)]
+    z_far = dev(x, y, (z + 4) % 8, core)
     x_to = [dev((x + 1) % 4, y, z, core), dev((x + 3) % 4, y, z, core)]
-    x_far = dev((x + 2) % 4, y, z, core)
 
     def rc(src, dst, ss, rs, d):
         return pltpu.make_async_remote_copy(
@@ -76,19 +75,31 @@
     ]
     for c in copies:
         c.start()
-    w_local = pltpu.make_async_copy(w_hbm, wbuf.at[y, core, x], lsem.at[2])
-
-    @pl.when(x == p)
+    w_local = pltpu.make_async_copy(w_hbm, wbuf.at[x, core, y], lsem.at[2])
+    w_stays = (x == p) & (y == x)
+
+    @pl.when(w_stays)
     def _():
         w_local.start()
 
     barrier = pltpu.get_barrier_semaphore()
-    partners = [sib, *y_to, z_up, z_dn, *z_two, *x_to, x_far]
+    partners = [sib, *y_to, z_up, z_dn, z_far, *x_to]
     for d in partners:
         pl.semaphore_signal(barrier, inc=1, device_id=d, device_id_type=MESH)
+
+    @pl.when(jnp.logical_not(w_stays))
+    def _():
+        pl.semaphore_signal(barrier, inc=1, device_id=dev(p, x, z, core), device_id_type=MESH)
+
+    for yy in range(4):
+        @pl.when((x == p) & ((y != x) | (yy != y)))
+        def _(yy=yy):
+            pl.semaphore_signal(barrier, inc=1, device_id=dev(y, yy, z, core), device_id_type=MESH)
+
     for c in copies:
         c.wait()
-    pl.semaphore_wait(barrier, len(partners))
+    holds = jnp.where(x == p, 4, 0) + jnp.where(w_stays, -1, 1)
+    pl.semaphore_wait(barrier, len(partners) + holds)
 
     def z_send(t):
         return rc(chunk(p - t, y, core), chunk(p - t, y, core), zs.at[t], zr.at[t + 1], z_up)
@@ -146,18 +157,25 @@
             c_send(t, 2).start()
 
     def w_move():
-        return rc(w_hbm, wbuf.at[y, core, x], wxs.at[0], wxr.at[x], dev(p, y, z, core))
+        return rc(w_hbm, wbuf.at[x, core, y], wxs.at[0], wxr.at[y], dev(p, x, z, core))
+
+    def w_order(i):
+        return (i + 2 * (1 - zh)) % 4
 
     def wz_send(i, d):
-        c = wbuf.at[y, core, i]
+        c = wbuf.at[y, core, w_order(i)]
         return rc(c, c, wzs.at[d, i], wzr.at[i], z_up if d == 0 else z_dn)
 
     def w_pass(i):
-        c = wbuf.at[y, core, i]
-
-        @pl.when((x == p) & (x != i))
-        def _():
-            rc(c, c, wxs.at[0], wxr.at[i], sib).wait_recv()
+        c = wbuf.at[y, core, w_order(i)]
+
+        @pl.when((x == p) & (y == x) & (w_order(i) == y))
+        def _():
+            w_local.wait()
+
+        @pl.when((x == p) & ((y != x) | (w_order(i) != y)))
+        def _():
+            rc(c, c, wxs.at[0], wxr.at[w_order(i)], sib).wait_recv()
 
         @pl.when(x != p)
         def _():
@@ -171,19 +189,50 @@
         def _():
             wz_send(i, 1).start()
 
-    def wy(yy, d, ss, rs):
-        c = wbuf.at[yy, core]
-        return rc(c, c, ss, rs, y_to[d])
-
-    def wy_half(yy, d):
-        c = wbuf.at[yy, core, pl.ds(2 * d, 2)]
-        return rc(c, c, wys2.at[d], wyr2.at[d], y_to[d])
-
-    def wc(off, c_):
-        c = wbuf.at[(y + off) % 4, c_]
-        return rc(c, c, wcs.at[off], wcr.at[off], sib)
-
-    @pl.when(x != p)
+    def w_half(yy, c_, k):
+        return wbuf.at[yy, c_, pl.ds(2 * ((1 - zh + k) % 2), 2)]
+
+    def wy_send(k, d):
+        c = w_half(y, core, k)
+        return rc(c, c, wys.at[d, k], wyr.at[d, k], y_to[d])
+
+    def wy_got(k, d):
+        c = w_half((y + 3 - 2 * d) % 4, core, k)
+        return rc(c, c, wys.at[d, k], wyr.at[d, k], y_to[d])
+
+    def wy_next(k, d):
+        c = wbuf.at[(y + 3 - 2 * d) % 4, core, 2 * ((1 - zh + k) % 2) + d]
+        return rc(c, c, wys2.at[d, k], wyr2.at[d, k], y_to[d])
+
+    def wy_far(k, d):
+        c = wbuf.at[(y + 2) % 4, core, 2 * ((1 - zh + k) % 2) + d]
+        return rc(c, c, wys2.at[d, k], wyr2.at[d, k], y_to[d])
+
+    def wc(k, off, c_):
+        c = w_half((y + off) % 4, c_, k)
+        return rc(c, c, wcs.at[k, off], wcr.at[k, off], sib)
+
+    def w_enter(k):
+        for d in range(2):
+            wy_send(k, d).start()
+        wc(k, 0, core).start()
+
+    def w_onward(k):
+        for d in range(2):
+            wy_got(k, d).wait_recv()
+            wy_next(k, d).start()
+            wc(k, 3 - 2 * d, core).start()
+
+    def w_finish(k):
+        for d in range(2):
+            wy_far(k, d).wait_recv()
+        wc(k, 2, core).start()
+
+    def w_done(k):
+        for off in range(4):
+            wc(k, off, 1 - core).wait_recv()
+
+    @pl.when(jnp.logical_not(w_stays))
     def _():
         w_move().start()
 
@@ -198,7 +247,7 @@
         d = 4 * BLOCK + i - j
         b = jnp.where(d == 0, 0.0, NEG)
         for e in range(NS):
-            b = jnp.where(d == slash[kv * GROUP + m, e] + 1, 0.0, b)
+            b = jnp.where(d == slash[e, kv * GROUP + m] + 1, 0.0, b)
         sbias[m, pl.ds(pl.multiple_of(strip * 32, 32), 32), :] = b
         return carry
 
@@ -207,34 +256,29 @@
     enter(1)
     onward(0)
     enter(2)
+    w_pass(0)
     onward(1)
     finish(0)
+    w_pass(1)
     enter(3)
+    w_pass(2)
+    w_pass(3)
     onward(2)
     finish(1)
-
-    @pl.when(x == p)
-    def _():
-        w_local.wait()
-
-    for i in range(4):
-        w_pass(i)
     onward(3)
+    w_enter(0)
     finish(2)
     finish(3)
+    w_enter(1)
     for t in range(4):
         @pl.when(p >= t)
         def _(t=t):
             for off in range(4):
                 c_got(t, off).wait_recv()
 
-    for d in range(2):
-        wy(y, d, wys.at[d], wyr.at[d]).start()
-    wc(0, core).start()
-
     def gather(m, carry):
         for j in range(NPICK):
-            b = 0 if j == 0 else vert[kv * GROUP + m, j - 1] + 1
+            b = 0 if j == 0 else vert[j - 1, kv * GROUP + m] + 1
             at = 4 + (0 if j == 0 else jnp.where(b < 4 * seq + 4, b, 0))
             kcat[m, j * BLOCK : (j + 1) * BLOCK, :] = kvbuf[at, 0]
             vcat[m, j * BLOCK : (j + 1) * BLOCK, :] = kvbuf[at, 1]
@@ -258,7 +302,7 @@
             oncol = bcol <= 0
             pb = [jnp.full((1, BLOCK), jnp.where(here > 0, 0.0, NEG), jnp.float32)]
             for e in range(NV):
-                b = vert[kv * GROUP + m, e] + 1
+                b = vert[e, kv * GROUP + m] + 1
                 oncol = oncol | (bcol == b)
                 pb.append(jnp.full((1, BLOCK), jnp.where(b < here, 0.0, NEG), jnp.float32))
             alt = jnp.where((wj >= 4 * BLOCK) & (wi >= wj - 4 * BLOCK), 0.0, NEG)
@@ -298,18 +342,15 @@
         return rc(c, c, xs2.at[d, r], xr2.at[d, r], x_to[d])
 
     def e_send(r, d):
-        src = zsrc.at[r, pl.ds(d * 64, 64)]
-        return rc(src, relay.at[r, d], es.at[d, r], er.at[d, r], z_two[d])
-
-    def f_send(r, d):
-        return rc(relay.at[r, d], zdst.at[r, pl.ds(d * 64, 64)], fs.at[d, r], fr.at[d, r], z_two[d])
+        c = pl.ds(d * 64, 64)
+        return rc(zsrc.at[r, c], zdst.at[r, c], es.at[d, r], er.at[d, r], z_far)
 
     def product(r, h):
         rows = pl.ds(pl.multiple_of(r * BLOCK, BLOCK), BLOCK)
         acc = None
         for i in range(4):
             w = jnp.concatenate(
-                [wbuf[2 * h + n // 2, n % 2, i] for n in range(4)], axis=1
+                [wbuf[i, n % 2, 2 * h + n // 2] for n in range(4)], axis=1
             )
             part = dot(abuf[i, rows, :], w)
             acc = part if acc is None else acc + part
@@ -324,19 +365,21 @@
 
         @pl.when(it == 1)
         def _():
-            for d in range(2):
-                yy = (y + 3 - 2 * d) % 4
-                wy(yy, d, wys.at[d], wyr.at[d]).wait_recv()
-                wy_half(yy, d).start()
-                wc(3 - 2 * d, core).start()
+            w_onward(0)
 
         @pl.when(it == 2)
         def _():
-            for d in range(2):
-                wy_half((y + 2) % 4, d).wait_recv()
-            wc(2, core).start()
-            for off in range(4):
-                wc(off, 1 - core).wait_recv()
+            w_finish(0)
+            w_done(0)
+            w_onward(1)
+
+        @pl.when(it == 3)
+        def _():
+            w_finish(1)
+
+        @pl.when(it == 4)
+        def _():
+            w_done(1)
 
         @pl.when((it >= 1) & (it < 5))
         def _():
@@ -352,21 +395,15 @@
             zsrc[r] = product(r, 1 - zh).astype(jnp.bfloat16)
             for d in range(2):
                 e_send(r, d).start()
-            own[r] = product(r, zh)
-
-        @pl.when((it >= 3) & (it < 7))
-        def _():
-            for d in range(2):
-                e_send(it - 3, d).wait_recv()
-                f_send(it - 3, d).start()
 
         @pl.when(it >= 4)
         def _():
             r = it - 4
-            for d in range(2):
-                f_send(r, d).wait_recv()
+            own = product(r, zh)
+            for d in range(2):
+                e_send(r, d).wait_recv()
             rows = pl.ds(pl.multiple_of(r * BLOCK, BLOCK), BLOCK)
-            out_ref[rows, :] = (own[r] + zdst[r].astype(jnp.float32)).astype(jnp.bfloat16)
+            out_ref[rows, :] = (own + zdst[r].astype(jnp.float32)).astype(jnp.bfloat16)
 
         return carry
 
@@ -385,7 +422,7 @@
             for off in range(4):
                 c_send(t, off).wait_send()
 
-    @pl.when(x != p)
+    @pl.when(jnp.logical_not(w_stays))
     def _():
         w_move().wait_send()
 
@@ -398,18 +435,18 @@
         def _(i=i):
             wz_send(i, 1).wait_send()
 
-    for d in range(2):
-        wy(y, d, wys.at[d], wyr.at[d]).wait_send()
-        wy_half((y + 3 - 2 * d) % 4, d).wait_send()
-    for off in range(4):
-        wc(off, core).wait_send()
+    for k in range(2):
+        for d in range(2):
+            wy_send(k, d).wait_send()
+            wy_next(k, d).wait_send()
+        for off in range(4):
+            wc(k, off, core).wait_send()
 
     def drain(r, carry):
         for d in range(2):
             x_send(r, d).wait_send()
             x_next(r, d).wait_send()
             e_send(r, d).wait_send()
-            f_send(r, d).wait_send()
         return carry
 
     lax.fori_loop(0, 4, drain, 0)
@@ -433,9 +470,7 @@
             pltpu.VMEM((GROUP, PICK, HEAD_DIM), bf16),
             pltpu.VMEM((GROUP, PICK, HEAD_DIM), bf16),
             pltpu.VMEM((GROUP, BLOCK, WIN), jnp.float32),
-            pltpu.VMEM((RBLK, BLOCK, ROWS), jnp.float32),
             pltpu.VMEM((RBLK, BLOCK, ROWS), bf16),
-            pltpu.VMEM((RBLK, 2, 64, ROWS), bf16),
             pltpu.VMEM((RBLK, BLOCK, ROWS), bf16),
             dma((3,)),
             dma((4,)), dma((4,)),
@@ -443,17 +478,17 @@
             dma((4, 4)), dma((4, 4)),
             dma((1,)), dma((4,)),
             dma((2, 4)), dma((4,)),
-            dma((2,)), dma((2,)), dma((2,)), dma((2,)),
-            dma((4,)), dma((4,)),
+            dma((2, 2)), dma((2, 2)), dma((2, 2)), dma((2, 2)),
+            dma((2, 4)), dma((2, 4)),
             dma((2, 4)), dma((2, 4)), dma((2, 4)), dma((2, 4)),
-            dma((2, 4)), dma((2, 4)), dma((2, 4)), dma((2, 4)),
+            dma((2, 4)), dma((2, 4)),
         ],
         compiler_params=pltpu.CompilerParams(
             collective_id=0, has_side_effects=True, vmem_limit_bytes=56 * 1024 * 1024
         ),
     )(
-        vertical,
-        slash_offsets,
+        vertical.T,
+        slash_offsets.T,
         queries,
         key_rows.reshape(4, BLOCK, HEAD_DIM),
         value_rows.reshape(4, BLOCK, HEAD_DIM),

time: 108 us -> 95.8 us (0.89)
  the two profiles are of different devices: /device:TPU:13 before, /device:TPU:97 now
where the time goes in v2:
time: 95.8 us; the launch traced here: 94.4 us
  Pallas kernels  92.5 us (97%)
  local copies, waits for them, and re-layouts  1.87 us (2%)
    pallas_call x1, Pallas kernels, shards(): pl.pallas_call(kernel, out_shape=jax.ShapeDtypeStruct((ROWS, ROWS), bf16)...  92.5 us

profile of v2, /device:TPU:97, one launch (start us, length us, event | category | flops | bytes accessed | tf_op | source)
XLA Modules:
  0.0 94.4 jit_solution(18427525791403116725)
XLA Ops:
  0.0 92.5 %shard_map.64 = bf16[512,512]{1,0:T(8,128)(2,1)} custom-call(s32[16,32]{1,0:T(8,128)} %bitcast.6, s32[16,32]{1,0:T(8,128)} %bitcast.7, bf16[512,512]{1,0:T(8,128)(2,1)} %q_ref.1, bf16[4,128,128]{2,1,0:T(8,128)(2,1)} %bitcast.4, bf16[4,128,128]{2,1,0:T(8,128)(2,1)} %bitcast.5, bf16[512,128]{1,0:T(8,128)(2,1)} %w_hbm.1), custom_call_target="tpu_custom_call" | custom-call | tf_op jit(solution)/shard_map/pallas_call | solution.py:461
  92.6 1.9 %copy.8 = bf16[512,512]{1,0:T(8,128)(2,1)} copy(bf16[512,512]{1,0:T(8,128)(2,1)} %shard_map.64) | data formatting | bytes 1048576

commit v3 on v2

--- a/solution.py
+++ b/solution.py
@@ -20,6 +20,11 @@
 WIN = 5 * BLOCK
 PICK = NPICK * BLOCK
 NEG = -1e30
+UNIT = 2
+LAG1 = 1
+LAG2 = 2
+LAG3 = 4
+W_STEPS = [(1, 0, 0), (2, 1, 0), (2, 2, 0), (2, 0, 1), (3, 1, 1), (4, 2, 1)]
 SCALE = math.log2(math.e) / math.sqrt(HEAD_DIM)
 
 
@@ -33,7 +38,7 @@
 
 def kernel(
     vert, slash, q_ref, k_hbm, v_hbm, w_hbm, out_ref,
-    kvbuf, wbuf, abuf, kcat, vcat, sbias, zsrc, zdst,
+    kvbuf, wbuf, abuf, sbias, zsrc, zdst,
     lsem, zs, zr, ys, yr, ys2, yr2, cs, cr,
     wxs, wxr, wzs, wzr, wys, wyr, wys2, wyr2, wcs, wcr,
     xs, xr, xs2, xr2, es, er,
@@ -189,6 +194,14 @@
         def _():
             wz_send(i, 1).start()
 
+    def w_pass_all():
+        for i in range(4):
+            w_pass(i)
+
+    def w_take(i):
+        c = wbuf.at[y, core, w_order(i)]
+        rc(c, c, wzs.at[0, i], wzr.at[i], sib).wait_recv()
+
     def w_half(yy, c_, k):
         return wbuf.at[yy, c_, pl.ds(2 * ((1 - zh + k) % 2), 2)]
 
@@ -253,22 +266,44 @@
 
     lax.fori_loop(0, 16, mask_step, 0)
 
+    @pl.when((p == 0) | ((p == 3) & (x == 3)))
+    def _():
+        w_pass_all()
+
     enter(1)
+
+    @pl.when(p == 1)
+    def _():
+        w_pass_all()
+
     onward(0)
     enter(2)
-    w_pass(0)
+
+    @pl.when(p == 2)
+    def _():
+        w_pass_all()
+
     onward(1)
     finish(0)
-    w_pass(1)
     enter(3)
-    w_pass(2)
-    w_pass(3)
     onward(2)
     finish(1)
     onward(3)
+
+    @pl.when((p == 3) & (x < 3))
+    def _():
+        w_take(0)
+        w_take(1)
+
     w_enter(0)
     finish(2)
     finish(3)
+
+    @pl.when((p == 3) & (x < 3))
+    def _():
+        w_take(2)
+        w_take(3)
+
     w_enter(1)
     for t in range(4):
         @pl.when(p >= t)
@@ -276,16 +311,6 @@
             for off in range(4):
                 c_got(t, off).wait_recv()
 
-    def gather(m, carry):
-        for j in range(NPICK):
-            b = 0 if j == 0 else vert[j - 1, kv * GROUP + m] + 1
-            at = 4 + (0 if j == 0 else jnp.where(b < 4 * seq + 4, b, 0))
-            kcat[m, j * BLOCK : (j + 1) * BLOCK, :] = kvbuf[at, 0]
-            vcat[m, j * BLOCK : (j + 1) * BLOCK, :] = kvbuf[at, 1]
-        return carry
-
-    lax.fori_loop(0, GROUP, gather, 0)
-
     wi = lax.broadcasted_iota(jnp.int32, (BLOCK, WIN), 0)
     wj = lax.broadcasted_iota(jnp.int32, (BLOCK, WIN), 1)
     lane = lax.broadcasted_iota(jnp.int32, (1, WIN), 1)
@@ -293,121 +318,117 @@
     def attend(r):
         rows = pl.ds(pl.multiple_of(r * BLOCK, BLOCK), BLOCK)
         here = 4 * seq + r
+        kw = kvbuf[pl.ds(here, 5), 0].reshape(WIN, HEAD_DIM)
+        vw = kvbuf[pl.ds(here, 5), 1].reshape(WIN, HEAD_DIM)
+        vw = jnp.concatenate([vw, jnp.ones((WIN, HEAD_DIM), jnp.bfloat16)], axis=1)
+        ones = jnp.ones((PICK, HEAD_DIM), jnp.bfloat16)
+        bcol = here - 4 + lane // BLOCK
+        alt = jnp.where((wj >= 4 * BLOCK) & (wi >= wj - 4 * BLOCK), 0.0, NEG)
         for m in range(GROUP):
-            cols = slice(m * HEAD_DIM, (m + 1) * HEAD_DIM)
-            q = q_ref[rows, cols]
-            kw = kvbuf[pl.ds(here, 5), 0].reshape(WIN, HEAD_DIM)
-            vw = kvbuf[pl.ds(here, 5), 1].reshape(WIN, HEAD_DIM)
-            bcol = here - 4 + lane // BLOCK
+            q = q_ref[rows, m * HEAD_DIM : (m + 1) * HEAD_DIM]
             oncol = bcol <= 0
             pb = [jnp.full((1, BLOCK), jnp.where(here > 0, 0.0, NEG), jnp.float32)]
+            at = [4]
             for e in range(NV):
                 b = vert[e, kv * GROUP + m] + 1
                 oncol = oncol | (bcol == b)
                 pb.append(jnp.full((1, BLOCK), jnp.where(b < here, 0.0, NEG), jnp.float32))
-            alt = jnp.where((wj >= 4 * BLOCK) & (wi >= wj - 4 * BLOCK), 0.0, NEG)
-            bias = jnp.where(oncol, alt, sbias[m])
-            sw = dot_t(q, kw) + bias
-            sp = dot_t(q, kcat[m]) + jnp.concatenate(pb, axis=1)
+                at.append(4 + jnp.where(b < here, b, 0))
+            kp = jnp.concatenate([kvbuf[a, 0] for a in at], axis=0)
+            vp = jnp.concatenate([kvbuf[a, 1] for a in at], axis=0)
+            sw = dot_t(q, kw) + jnp.where(oncol, alt, sbias[m])
+            sp = dot_t(q, kp) + jnp.concatenate(pb, axis=1)
             peak = jnp.maximum(
                 jnp.max(sw, axis=1, keepdims=True), jnp.max(sp, axis=1, keepdims=True)
             )
             pw = jnp.exp2((sw - peak) * SCALE).astype(jnp.bfloat16)
             pp = jnp.exp2((sp - peak) * SCALE).astype(jnp.bfloat16)
-            ones_w = jnp.ones((WIN, HEAD_DIM), jnp.bfloat16)
-            ones_p = jnp.ones((PICK, HEAD_DIM), jnp.bfloat16)
-            o = dot(pw, jnp.concatenate([vw, ones_w], axis=1))
-            o = o + dot(pp, jnp.concatenate([vcat[m], ones_p], axis=1))
-            abuf[x, rows, cols] = (o[:, :HEAD_DIM] / o[:, HEAD_DIM:]).astype(jnp.bfloat16)
-
-    def a_part(xx, r):
-        return abuf.at[xx, pl.ds(pl.multiple_of(r * BLOCK, BLOCK), BLOCK)]
-
-    def a_half(xx, r, d):
-        return abuf.at[xx, pl.ds(pl.multiple_of(r * BLOCK + d * 64, 64), 64)]
-
-    def x_send(r, d):
-        return rc(a_part(x, r), a_part(x, r), xs.at[d, r], xr.at[d, r], x_to[d])
-
-    def x_got(r, d):
-        c = a_part((x + 3 - 2 * d) % 4, r)
-        return rc(c, c, xs.at[d, r], xr.at[d, r], x_to[d])
-
-    def x_next(r, d):
-        c = a_half((x + 3 - 2 * d) % 4, r, d)
-        return rc(c, c, xs2.at[d, r], xr2.at[d, r], x_to[d])
-
-    def x_last(r, d):
-        c = a_half((x + 2) % 4, r, d)
-        return rc(c, c, xs2.at[d, r], xr2.at[d, r], x_to[d])
+            o = dot(pw, vw) + dot(pp, jnp.concatenate([vp, ones], axis=1))
+            abuf[x, r, m] = (o[:, :HEAD_DIM] / o[:, HEAD_DIM:]).astype(jnp.bfloat16)
+
+    def a_part(xx, r, m):
+        return abuf.at[xx, r, pl.ds(m - UNIT + 1, UNIT)]
+
+    def a_half(xx, r, m, d):
+        if UNIT > 1:
+            return abuf.at[xx, r, pl.ds(m - UNIT + 1 + d * (UNIT // 2), UNIT // 2)]
+        return abuf.at[xx, r, m, pl.ds(d * 64, 64)]
+
+    def x_copy(c, ss, rs, r, m, d):
+        n = r * GROUP + m
+        return rc(c, c, ss.at[d, n], rs.at[d, n], x_to[d])
+
+    def x_send(r, m, d):
+        return x_copy(a_part(x, r, m), xs, xr, r, m, d)
+
+    def x_got(r, m, d):
+        return x_copy(a_part((x + 3 - 2 * d) % 4, r, m), xs, xr, r, m, d)
+
+    def x_next(r, m, d):
+        return x_copy(a_half((x + 3 - 2 * d) % 4, r, m, d), xs2, xr2, r, m, d)
+
+    def x_last(r, m, d):
+        return x_copy(a_half((x + 2) % 4, r, m, d), xs2, xr2, r, m, d)
 
     def e_send(r, d):
         c = pl.ds(d * 64, 64)
         return rc(zsrc.at[r, c], zdst.at[r, c], es.at[d, r], er.at[d, r], z_far)
 
     def product(r, h):
-        rows = pl.ds(pl.multiple_of(r * BLOCK, BLOCK), BLOCK)
         acc = None
         for i in range(4):
             w = jnp.concatenate(
                 [wbuf[i, n % 2, 2 * h + n // 2] for n in range(4)], axis=1
             )
-            part = dot(abuf[i, rows, :], w)
+            a = jnp.concatenate([abuf[i, r, m] for m in range(GROUP)], axis=1)
+            part = dot(a, w)
             acc = part if acc is None else acc + part
         return acc
 
+    ends = range(UNIT - 1, GROUP, UNIT)
+
     def step(it, carry):
-        @pl.when(it < 4)
+        @pl.when(it < RBLK)
         def _():
             attend(it)
-            for d in range(2):
-                x_send(it, d).start()
-
-        @pl.when(it == 1)
-        def _():
-            w_onward(0)
-
-        @pl.when(it == 2)
-        def _():
-            w_finish(0)
-            w_done(0)
-            w_onward(1)
-
-        @pl.when(it == 3)
-        def _():
-            w_finish(1)
-
-        @pl.when(it == 4)
-        def _():
-            w_done(1)
-
-        @pl.when((it >= 1) & (it < 5))
-        def _():
-            for d in range(2):
-                x_got(it - 1, d).wait_recv()
-                x_next(it - 1, d).start()
-
-        @pl.when((it >= 2) & (it < 6))
-        def _():
-            r = it - 2
-            for d in range(2):
-                x_last(r, d).wait_recv()
+            for m in ends:
+                for d in range(2):
+                    x_send(it, m, d).start()
+
+        for at, act, k in W_STEPS:
+            @pl.when(it == at)
+            def _(act=act, k=k):
+                (w_onward, w_finish, w_done)[act](k)
+
+        @pl.when((it >= LAG1) & (it < RBLK + LAG1))
+        def _():
+            for m in ends:
+                for d in range(2):
+                    x_got(it - LAG1, m, d).wait_recv()
+                    x_next(it - LAG1, m, d).start()
+
+        @pl.when((it >= LAG2) & (it < RBLK + LAG2))
+        def _():
+            r = it - LAG2
+            for m in ends:
+                for d in range(2):
+                    x_last(r, m, d).wait_recv()
             zsrc[r] = product(r, 1 - zh).astype(jnp.bfloat16)
             for d in range(2):
                 e_send(r, d).start()
 
-        @pl.when(it >= 4)
-        def _():
-            r = it - 4
-            own = product(r, zh)
+        @pl.when(it >= LAG3)
+        def _():
+            r = it - LAG3
+            mine = product(r, zh)
             for d in range(2):
                 e_send(r, d).wait_recv()
             rows = pl.ds(pl.multiple_of(r * BLOCK, BLOCK), BLOCK)
-            out_ref[rows, :] = (own + zdst[r].astype(jnp.float32)).astype(jnp.bfloat16)
+            out_ref[rows, :] = (mine + zdst[r].astype(jnp.float32)).astype(jnp.bfloat16)
 
         return carry
 
-    lax.fori_loop(0, 8, step, 0)
+    lax.fori_loop(0, RBLK + LAG3, step, 0)
 
     for t in range(4):
         @pl.when(p >= t)
@@ -444,8 +465,9 @@
 
     def drain(r, carry):
         for d in range(2):
-            x_send(r, d).wait_send()
-            x_next(r, d).wait_send()
+            for m in range(UNIT - 1, GROUP, UNIT):
+                x_send(r, m, d).wait_send()
+                x_next(r, m, d).wait_send()
             e_send(r, d).wait_send()
         return carry
 
@@ -466,9 +488,7 @@
         scratch_shapes=[
             pltpu.VMEM((132, 2, BLOCK, HEAD_DIM), bf16),
             pltpu.VMEM((4, 2, 4, ROWS, 128), bf16),
-            pltpu.VMEM((4, ROWS, ROWS), bf16),
-            pltpu.VMEM((GROUP, PICK, HEAD_DIM), bf16),
-            pltpu.VMEM((GROUP, PICK, HEAD_DIM), bf16),
+            pltpu.VMEM((4, RBLK, GROUP, BLOCK, HEAD_DIM), bf16),
             pltpu.VMEM((GROUP, BLOCK, WIN), jnp.float32),
             pltpu.VMEM((RBLK, BLOCK, ROWS), bf16),
             pltpu.VMEM((RBLK, BLOCK, ROWS), bf16),
@@ -480,7 +500,7 @@
             dma((2, 4)), dma((4,)),
             dma((2, 2)), dma((2, 2)), dma((2, 2)), dma((2, 2)),
             dma((2, 4)), dma((2, 4)),
-            dma((2, 4)), dma((2, 4)), dma((2, 4)), dma((2, 4)),
+            dma((2, 16)), dma((2, 16)), dma((2, 16)), dma((2, 16)),
             dma((2, 4)), dma((2, 4)),
         ],
         compiler_params=pltpu.CompilerParams(

time: 95.8 us -> 90.3 us (0.943); the launches traced: 94.4 us -> 90.2 us
  Pallas kernels: 92.5 us -> 88.3 us
    pallas_call x1, Pallas kernels: 92.5 us -> 88.3 us  [shards(): pl.pallas_call(kernel, out_shape=jax.ShapeDtypeStruct((ROWS, ROWS), bf16)...]
where the time goes in v3:
time: 90.3 us; the launch traced here: 90.2 us
  Pallas kernels  88.3 us (98%)
  local copies, waits for them, and re-layouts  1.87 us (2%)
    pallas_call x1, Pallas kernels, shards(): pl.pallas_call(kernel, out_shape=jax.ShapeDtypeStruct((ROWS, ROWS), bf16)...  88.3 us
    unnamed x1, local copies, waits for them, and re-layouts  1.87 us

profile of v3, /device:TPU:97, one launch (start us, length us, event | category | flops | bytes accessed | tf_op | source)
XLA Modules:
  0.0 90.2 jit_solution(9894463646959016738)
XLA Ops:
  0.0 88.3 %shard_map.64 = bf16[512,512]{1,0:T(8,128)(2,1)} custom-call(s32[16,32]{1,0:T(8,128)} %bitcast.6, s32[16,32]{1,0:T(8,128)} %bitcast.7, bf16[512,512]{1,0:T(8,128)(2,1)} %q_ref.1, bf16[4,128,128]{2,1,0:T(8,128)(2,1)} %bitcast.4, bf16[4,128,128]{2,1,0:T(8,128)(2,1)} %bitcast.5, bf16[512,128]{1,0:T(8,128)(2,1)} %w_hbm.1), custom_call_target="tpu_custom_call" | custom-call | tf_op jit(solution)/shard_map/pallas_call | solution.py:483
  88.3 1.9 %copy.8 = bf16[512,512]{1,0:T(8,128)(2,1)} copy(bf16[512,512]{1,0:T(8,128)(2,1)} %shard_map.64) | data formatting | bytes 1048576

commit v4 on v3

--- a/solution.py
+++ b/solution.py
@@ -21,10 +21,11 @@
 PICK = NPICK * BLOCK
 NEG = -1e30
 UNIT = 2
-LAG1 = 1
 LAG2 = 2
-LAG3 = 4
-W_STEPS = [(1, 0, 0), (2, 1, 0), (2, 2, 0), (2, 0, 1), (3, 1, 1), (4, 2, 1)]
+LAG3 = 6
+LATE = 0
+W_STEPS = [(1, 0, 0), (2, 1, 0), (2, 2, 0)]
+W_LATER = [(3, 0, 1), (4, 1, 1), (5, 2, 1)]
 SCALE = math.log2(math.e) / math.sqrt(HEAD_DIM)
 
 
@@ -39,7 +40,7 @@
 def kernel(
     vert, slash, q_ref, k_hbm, v_hbm, w_hbm, out_ref,
     kvbuf, wbuf, abuf, sbias, zsrc, zdst,
-    lsem, zs, zr, ys, yr, ys2, yr2, cs, cr,
+    lsem, zs, zr, zfs, zfr, ys, yr, ys2, yr2, cs, cr,
     wxs, wxr, wzs, wzr, wys, wyr, wys2, wyr2, wcs, wcr,
     xs, xr, xs2, xr2, es, er,
 ):
@@ -57,6 +58,8 @@
 
     sib = dev(x, y, z, 1 - core)
     y_to = [dev(x, (y + 1) % 4, z, core), dev(x, (y + 3) % 4, z, core)]
+    x_two = dev((x + 2) % 4, y, z, core)
+    y_two = dev(x, (y + 2) % 4, z, core)
     z_up = dev(x, y, (z + 1) % 8, core)
     z_dn = dev(x, y, (z + 7) % 8, core)
     z_far = dev(x, y, (z + 4) % 8, core)
@@ -88,7 +91,7 @@
         w_local.start()
 
     barrier = pltpu.get_barrier_semaphore()
-    partners = [sib, *y_to, z_up, z_dn, z_far, *x_to]
+    partners = [sib, *y_to, z_up, z_dn, z_far, *x_to, x_two, y_two]
     for d in partners:
         pl.semaphore_signal(barrier, inc=1, device_id=d, device_id_type=MESH)
 
@@ -131,6 +134,22 @@
     def c_got(t, off):
         c = chunk(p - t, (y + off) % 4, 1 - core)
         return rc(c, c, cs.at[t, off], cr.at[t, off], sib)
+
+    filled = (p == 3) & (x == 3)
+
+    def z_fill(n):
+        c = chunk(2, (y + 2) % 4, core) if n == 2 else half(2, (y + 3 - 2 * n) % 4, core, 1 - n)
+        return rc(c, c, zfs.at[n], zfr.at[n], z_up)
+
+    def y_part(yy, d):
+        c = half(2, yy, core, d)
+        return rc(c, c, ys.at[d, 1], yr.at[d, 1], y_to[d])
+
+    def fill():
+        @pl.when((p == 2) & (x == 3))
+        def _():
+            for n in range(3):
+                z_fill(n).start()
 
     def enter(t):
         @pl.when(p >= t)
@@ -142,12 +161,24 @@
                 @pl.when(p < 3)
                 def _():
                     z_send(t).start()
-            for d in range(2):
-                y_send(t, d).start()
             c_send(t, 0).start()
+            if t != 1:
+                for d in range(2):
+                    y_send(t, d).start()
+
+        if t == 1:
+            @pl.when((p >= 1) & jnp.logical_not(filled))
+            def _():
+                for d in range(2):
+                    y_send(t, d).start()
+
+            @pl.when(filled)
+            def _():
+                for d in range(2):
+                    y_part(y, d).start()
 
     def onward(t):
-        @pl.when(p >= t)
+        @pl.when((p >= t) & (jnp.logical_not(filled) | (t != 1)))
         def _():
             for d in range(2):
                 y_got(t, d).wait_recv()
@@ -155,12 +186,22 @@
                 c_send(t, 3 - 2 * d).start()
 
     def finish(t):
-        @pl.when(p >= t)
+        @pl.when((p >= t) & (jnp.logical_not(filled) | (t != 1)))
         def _():
             for d in range(2):
                 y_far(t, d).wait_recv()
             c_send(t, 2).start()
 
+    def fill_take():
+        @pl.when(filled)
+        def _():
+            for d in range(2):
+                y_part((y + 3 - 2 * d) % 4, d).wait_recv()
+                z_fill(d).wait_recv()
+                c_send(1, 3 - 2 * d).start()
+            z_fill(2).wait_recv()
+            c_send(1, 2).start()
+
     def w_move():
         return rc(w_hbm, wbuf.at[x, core, y], wxs.at[0], wxr.at[y], dev(p, x, z, core))
 
@@ -194,8 +235,8 @@
         def _():
             wz_send(i, 1).start()
 
-    def w_pass_all():
-        for i in range(4):
+    def w_pass_some(first, last):
+        for i in range(first, last):
             w_pass(i)
 
     def w_take(i):
@@ -266,25 +307,34 @@
 
     lax.fori_loop(0, 16, mask_step, 0)
 
-    @pl.when((p == 0) | ((p == 3) & (x == 3)))
-    def _():
-        w_pass_all()
+    @pl.when(((p == 0) & (x == 0)) | ((p == 3) & (x == 3)))
+    def _():
+        w_pass_some(0, 4)
 
     enter(1)
 
     @pl.when(p == 1)
     def _():
-        w_pass_all()
+        w_pass_some(0, 4)
+
+    @pl.when((p == 2) & (x >= 2))
+    def _():
+        w_pass_some(0, 2)
 
     onward(0)
     enter(2)
 
-    @pl.when(p == 2)
-    def _():
-        w_pass_all()
+    @pl.when((p == 2) & (x >= 2))
+    def _():
+        w_pass_some(2, 4)
+
+    @pl.when((p == 2) & (x < 2))
+    def _():
+        w_pass_some(0, 4)
 
     onward(1)
     finish(0)
+    fill()
     enter(3)
     onward(2)
     finish(1)
@@ -295,7 +345,13 @@
         w_take(0)
         w_take(1)
 
-    w_enter(0)
+    fill_take()
+    w_late = (p == 0) & (x > 0)
+
+    @pl.when(jnp.logical_not(w_late))
+    def _():
+        w_enter(0)
+
     finish(2)
     finish(3)
 
@@ -304,7 +360,10 @@
         w_take(2)
         w_take(3)
 
-    w_enter(1)
+    @pl.when(jnp.logical_not(w_late))
+    def _():
+        w_enter(1)
+
     for t in range(4):
         @pl.when(p >= t)
         def _(t=t):
@@ -349,11 +408,6 @@
     def a_part(xx, r, m):
         return abuf.at[xx, r, pl.ds(m - UNIT + 1, UNIT)]
 
-    def a_half(xx, r, m, d):
-        if UNIT > 1:
-            return abuf.at[xx, r, pl.ds(m - UNIT + 1 + d * (UNIT // 2), UNIT // 2)]
-        return abuf.at[xx, r, m, pl.ds(d * 64, 64)]
-
     def x_copy(c, ss, rs, r, m, d):
         n = r * GROUP + m
         return rc(c, c, ss.at[d, n], rs.at[d, n], x_to[d])
@@ -364,11 +418,10 @@
     def x_got(r, m, d):
         return x_copy(a_part((x + 3 - 2 * d) % 4, r, m), xs, xr, r, m, d)
 
-    def x_next(r, m, d):
-        return x_copy(a_half((x + 3 - 2 * d) % 4, r, m, d), xs2, xr2, r, m, d)
-
-    def x_last(r, m, d):
-        return x_copy(a_half((x + 2) % 4, r, m, d), xs2, xr2, r, m, d)
+    def x_far(xx, r, m):
+        c = a_part(xx, r, m)
+        n = r * GROUP + m
+        return rc(c, c, xs2.at[n], xr2.at[n], x_two)
 
     def e_send(r, d):
         c = pl.ds(d * 64, 64)
@@ -394,28 +447,37 @@
             for m in ends:
                 for d in range(2):
                     x_send(it, m, d).start()
+                x_far(x, it, m).start()
+
+        @pl.when((it == LATE) & w_late)
+        def _():
+            w_take(0)
+            w_take(1)
+            w_enter(0)
+            w_take(2)
+            w_take(3)
+            w_enter(1)
 
         for at, act, k in W_STEPS:
             @pl.when(it == at)
             def _(act=act, k=k):
                 (w_onward, w_finish, w_done)[act](k)
 
-        @pl.when((it >= LAG1) & (it < RBLK + LAG1))
-        def _():
-            for m in ends:
-                for d in range(2):
-                    x_got(it - LAG1, m, d).wait_recv()
-                    x_next(it - LAG1, m, d).start()
-
         @pl.when((it >= LAG2) & (it < RBLK + LAG2))
         def _():
             r = it - LAG2
             for m in ends:
                 for d in range(2):
-                    x_last(r, m, d).wait_recv()
+                    x_got(r, m, d).wait_recv()
+                x_far((x + 2) % 4, r, m).wait_recv()
             zsrc[r] = product(r, 1 - zh).astype(jnp.bfloat16)
             for d in range(2):
                 e_send(r, d).start()
+
+        for at, act, k in W_LATER:
+            @pl.when(it == at)
+            def _(act=act, k=k):
+                (w_onward, w_finish, w_done)[act](k)
 
         @pl.when(it >= LAG3)
         def _():
@@ -437,11 +499,24 @@
                 @pl.when(p < 3)
                 def _():
                     z_send(t).wait_send()
+            for off in range(4):
+                c_send(t, off).wait_send()
+
+        @pl.when((p >= t) & (jnp.logical_not(filled) | (t != 1)))
+        def _(t=t):
             for d in range(2):
                 y_send(t, d).wait_send()
                 y_next(t, d).wait_send()
-            for off in range(4):
-                c_send(t, off).wait_send()
+
+    @pl.when(filled)
+    def _():
+        for d in range(2):
+            y_part(y, d).wait_send()
+
+    @pl.when((p == 2) & (x == 3))
+    def _():
+        for n in range(3):
+            z_fill(n).wait_send()
 
     @pl.when(jnp.logical_not(w_stays))
     def _():
@@ -467,8 +542,9 @@
         for d in range(2):
             for m in range(UNIT - 1, GROUP, UNIT):
                 x_send(r, m, d).wait_send()
-                x_next(r, m, d).wait_send()
             e_send(r, d).wait_send()
+        for m in ends:
+            x_far(x, r, m).wait_send()
         return carry
 
     lax.fori_loop(0, 4, drain, 0)
@@ -493,14 +569,14 @@
             pltpu.VMEM((RBLK, BLOCK, ROWS), bf16),
             pltpu.VMEM((RBLK, BLOCK, ROWS), bf16),
             dma((3,)),
-            dma((4,)), dma((4,)),
+            dma((4,)), dma((4,)), dma((3,)), dma((3,)),
             dma((2, 4)), dma((2, 4)), dma((2, 4)), dma((2, 4)),
             dma((4, 4)), dma((4, 4)),
             dma((1,)), dma((4,)),
             dma((2, 4)), dma((4,)),
             dma((2, 2)), dma((2, 2)), dma((2, 2)), dma((2, 2)),
             dma((2, 4)), dma((2, 4)),
-            dma((2, 16)), dma((2, 16)), dma((2, 16)), dma((2, 16)),
+            dma((2, 16)), dma((2, 16)), dma((16,)), dma((16,)),
             dma((2, 4)), dma((2, 4)),
         ],
         compiler_params=pltpu.CompilerParams(

time: 90.3 us -> 88.5 us (0.980)
  Pallas kernels: 88.3 us -> 86.1 us
    pallas_call x1, Pallas kernels: 88.3 us -> 86.1 us  [shards(): pl.pallas_call(kernel, out_shape=jax.ShapeDtypeStruct((ROWS, ROWS), bf16)...]
where the time goes in v4:
time: 88.5 us; the launch traced here: 87.9 us
  Pallas kernels  86.1 us (97%)
  local copies, waits for them, and re-layouts  1.87 us (2%)
    pallas_call x1, Pallas kernels, shards(): pl.pallas_call(kernel, out_shape=jax.ShapeDtypeStruct((ROWS, ROWS), bf16)...  86.1 us
    unnamed x1, local copies, waits for them, and re-layouts  1.87 us

profile of v4, /device:TPU:97, one launch (start us, length us, event | category | flops | bytes accessed | tf_op | source)
XLA Modules:
  0.0 87.9 jit_solution(9334939672585339028)
XLA Ops:
  0.0 86.1 %shard_map.64 = bf16[512,512]{1,0:T(8,128)(2,1)} custom-call(s32[16,32]{1,0:T(8,128)} %bitcast.6, s32[16,32]{1,0:T(8,128)} %bitcast.7, bf16[512,512]{1,0:T(8,128)(2,1)} %q_ref.1, bf16[4,128,128]{2,1,0:T(8,128)(2,1)} %bitcast.4, bf16[4,128,128]{2,1,0:T(8,128)(2,1)} %bitcast.5, bf16[512,128]{1,0:T(8,128)(2,1)} %w_hbm.1), custom_call_target="tpu_custom_call" | custom-call | tf_op jit(solution)/shard_map/pallas_call | solution.py:559
  86.1 1.9 %copy.8 = bf16[512,512]{1,0:T(8,128)(2,1)} copy(bf16[512,512]{1,0:T(8,128)(2,1)} %shard_map.64) | data formatting | bytes 1048576

commit v5 on v4

--- a/solution.py
+++ b/solution.py
@@ -38,8 +38,8 @@
 
 
 def kernel(
-    vert, slash, q_ref, k_hbm, v_hbm, w_hbm, out_ref,
-    kvbuf, wbuf, abuf, sbias, zsrc, zdst,
+    vert, slash, q_hbm, k_hbm, v_hbm, w_hbm, out_ref,
+    q_ref, kvbuf, wbuf, abuf, sbias, zsrc, zdst,
     lsem, zs, zr, zfs, zfr, ys, yr, ys2, yr2, cs, cr,
     wxs, wxr, wzs, wzr, wys, wyr, wys2, wyr2, wcs, wcr,
     xs, xr, xs2, xr2, es, er,
@@ -59,7 +59,6 @@
     sib = dev(x, y, z, 1 - core)
     y_to = [dev(x, (y + 1) % 4, z, core), dev(x, (y + 3) % 4, z, core)]
     x_two = dev((x + 2) % 4, y, z, core)
-    y_two = dev(x, (y + 2) % 4, z, core)
     z_up = dev(x, y, (z + 1) % 8, core)
     z_dn = dev(x, y, (z + 7) % 8, core)
     z_far = dev(x, y, (z + 4) % 8, core)
@@ -83,6 +82,8 @@
     ]
     for c in copies:
         c.start()
+    q_copy = pltpu.make_async_copy(q_hbm, q_ref, lsem.at[3])
+    q_copy.start()
     w_local = pltpu.make_async_copy(w_hbm, wbuf.at[x, core, y], lsem.at[2])
     w_stays = (x == p) & (y == x)
 
@@ -91,7 +92,7 @@
         w_local.start()
 
     barrier = pltpu.get_barrier_semaphore()
-    partners = [sib, *y_to, z_up, z_dn, z_far, *x_to, x_two, y_two]
+    partners = [sib, *y_to, z_up, z_dn, z_far, *x_to, x_two]
     for d in partners:
         pl.semaphore_signal(barrier, inc=1, device_id=d, device_id_type=MESH)
 
@@ -138,17 +139,17 @@
     filled = (p == 3) & (x == 3)
 
     def z_fill(n):
-        c = chunk(2, (y + 2) % 4, core) if n == 2 else half(2, (y + 3 - 2 * n) % 4, core, 1 - n)
+        c = chunk(2, (y + (3, 1, 2)[n]) % 4, core)
         return rc(c, c, zfs.at[n], zfr.at[n], z_up)
 
-    def y_part(yy, d):
-        c = half(2, yy, core, d)
-        return rc(c, c, ys.at[d, 1], yr.at[d, 1], y_to[d])
-
     def fill():
+        @pl.when(p == 2)
+        def _():
+            z_fill(2).start()
+
         @pl.when((p == 2) & (x == 3))
         def _():
-            for n in range(3):
+            for n in range(2):
                 z_fill(n).start()
 
     def enter(t):
@@ -172,21 +173,20 @@
                 for d in range(2):
                     y_send(t, d).start()
 
-            @pl.when(filled)
-            def _():
-                for d in range(2):
-                    y_part(y, d).start()
-
     def onward(t):
         @pl.when((p >= t) & (jnp.logical_not(filled) | (t != 1)))
         def _():
             for d in range(2):
                 y_got(t, d).wait_recv()
-                y_next(t, d).start()
+
+                @pl.when((p < 3) | (t != 1))
+                def _(d=d):
+                    y_next(t, d).start()
+
                 c_send(t, 3 - 2 * d).start()
 
     def finish(t):
-        @pl.when((p >= t) & (jnp.logical_not(filled) | (t != 1)))
+        @pl.when((p >= t) & ((p < 3) | (t != 1)))
         def _():
             for d in range(2):
                 y_far(t, d).wait_recv()
@@ -196,9 +196,11 @@
         @pl.when(filled)
         def _():
             for d in range(2):
-                y_part((y + 3 - 2 * d) % 4, d).wait_recv()
                 z_fill(d).wait_recv()
                 c_send(1, 3 - 2 * d).start()
+
+        @pl.when(p == 3)
+        def _():
             z_fill(2).wait_recv()
             c_send(1, 2).start()
 
@@ -313,7 +315,7 @@
 
     enter(1)
 
-    @pl.when(p == 1)
+    @pl.when((p == 1) & (x < 2))
     def _():
         w_pass_some(0, 4)
 
@@ -334,6 +336,11 @@
 
     onward(1)
     finish(0)
+
+    @pl.when((p == 1) & (x >= 2))
+    def _():
+        w_pass_some(0, 4)
+
     fill()
     enter(3)
     onward(2)
@@ -370,6 +377,7 @@
             for off in range(4):
                 c_got(t, off).wait_recv()
 
+    q_copy.wait()
     wi = lax.broadcasted_iota(jnp.int32, (BLOCK, WIN), 0)
     wj = lax.broadcasted_iota(jnp.int32, (BLOCK, WIN), 1)
     lane = lax.broadcasted_iota(jnp.int32, (1, WIN), 1)
@@ -506,16 +514,19 @@
         def _(t=t):
             for d in range(2):
                 y_send(t, d).wait_send()
+
+        @pl.when((p >= t) & ((p < 3) | (t != 1)))
+        def _(t=t):
+            for d in range(2):
                 y_next(t, d).wait_send()
 
-    @pl.when(filled)
-    def _():
-        for d in range(2):
-            y_part(y, d).wait_send()
+    @pl.when(p == 2)
+    def _():
+        z_fill(2).wait_send()
 
     @pl.when((p == 2) & (x == 3))
     def _():
-        for n in range(3):
+        for n in range(2):
             z_fill(n).wait_send()
 
     @pl.when(jnp.logical_not(w_stays))
@@ -559,16 +570,17 @@
     return pl.pallas_call(
         kernel,
         out_shape=jax.ShapeDtypeStruct((ROWS, ROWS), bf16),
-        in_specs=[smem, smem, vmem, anyspace, anyspace, anyspace],
+        in_specs=[smem, smem, anyspace, anyspace, anyspace, anyspace],
         out_specs=vmem,
         scratch_shapes=[
+            pltpu.VMEM((ROWS, GROUP * HEAD_DIM), bf16),
             pltpu.VMEM((132, 2, BLOCK, HEAD_DIM), bf16),
             pltpu.VMEM((4, 2, 4, ROWS, 128), bf16),
             pltpu.VMEM((4, RBLK, GROUP, BLOCK, HEAD_DIM), bf16),
             pltpu.VMEM((GROUP, BLOCK, WIN), jnp.float32),
             pltpu.VMEM((RBLK, BLOCK, ROWS), bf16),
             pltpu.VMEM((RBLK, BLOCK, ROWS), bf16),
-            dma((3,)),
+            dma((4,)),
             dma((4,)), dma((4,)), dma((3,)), dma((3,)),
             dma((2, 4)), dma((2, 4)), dma((2, 4)), dma((2, 4)),
             dma((4, 4)), dma((4, 4)),

time: 88.5 us -> 86.2 us (0.974)
  Pallas kernels: 86.1 us -> 84.2 us
    pallas_call x1, Pallas kernels: 86.1 us -> 84.2 us  [shards(): pl.pallas_call(kernel, out_shape=jax.ShapeDtypeStruct((ROWS, ROWS), bf16)...]
where the time goes in v5:
time: 86.2 us; the launch traced here: 86.1 us
  Pallas kernels  84.2 us (98%)
  local copies, waits for them, and re-layouts  1.87 us (2%)
    pallas_call x1, Pallas kernels, shards(): pl.pallas_call(kernel, out_shape=jax.ShapeDtypeStruct((ROWS, ROWS), bf16)...  84.2 us
    unnamed x1, local copies, waits for them, and re-layouts  1.87 us

profile of v5, /device:TPU:97, one launch (start us, length us, event | category | flops | bytes accessed | tf_op | source)
XLA Modules:
  0.0 86.1 jit_solution(796818176284914)
XLA Ops:
  0.0 84.2 %shard_map.64 = bf16[512,512]{1,0:T(8,128)(2,1)} custom-call(s32[16,32]{1,0:T(8,128)} %bitcast.6, s32[16,32]{1,0:T(8,128)} %bitcast.7, bf16[512,512]{1,0:T(8,128)(2,1)} %q_hbm.1, bf16[4,128,128]{2,1,0:T(8,128)(2,1)} %bitcast.4, bf16[4,128,128]{2,1,0:T(8,128)(2,1)} %bitcast.5, bf16[512,128]{1,0:T(8,128)(2,1)} %w_hbm.1), custom_call_target="tpu_custom_call" | custom-call | tf_op jit(solution)/shard_map/pallas_call | solution.py:570
  84.2 1.9 %copy.8 = bf16[512,512]{1,0:T(8,128)(2,1)} copy(bf16[512,512]{1,0:T(8,128)(2,1)} %shard_map.64) | data formatting | bytes 1048576

commit v6 on v5

--- a/solution.py
+++ b/solution.py
@@ -20,7 +20,7 @@
 WIN = 5 * BLOCK
 PICK = NPICK * BLOCK
 NEG = -1e30
-UNIT = 2
+UNIT = 4
 LAG2 = 2
 LAG3 = 6
 LATE = 0
@@ -311,9 +311,13 @@
 
     @pl.when(((p == 0) & (x == 0)) | ((p == 3) & (x == 3)))
     def _():
-        w_pass_some(0, 4)
+        w_pass_some(0, 2)
 
     enter(1)
+
+    @pl.when(((p == 0) & (x == 0)) | ((p == 3) & (x == 3)))
+    def _():
+        w_pass_some(2, 4)
 
     @pl.when((p == 1) & (x < 2))
     def _():

time: 86.2 us -> 86.4 us (level)
  no operation moved by 1% of the time
where the time goes in v6:
time: 86.4 us; the launch traced here: 86.2 us
  Pallas kernels  84.3 us (98%)
  local copies, waits for them, and re-layouts  1.87 us (2%)
    pallas_call x1, Pallas kernels, shards(): pl.pallas_call(kernel, out_shape=jax.ShapeDtypeStruct((ROWS, ROWS), bf16)...  84.3 us
    unnamed x1, local copies, waits for them, and re-layouts  1.87 us

profile of v6, /device:TPU:97, one launch (start us, length us, event | category | flops | bytes accessed | tf_op | source)
XLA Modules:
  0.0 86.2 jit_solution(16705578804765509898)
XLA Ops:
  0.0 84.3 %shard_map.64 = bf16[512,512]{1,0:T(8,128)(2,1)} custom-call(s32[16,32]{1,0:T(8,128)} %bitcast.6, s32[16,32]{1,0:T(8,128)} %bitcast.7, bf16[512,512]{1,0:T(8,128)(2,1)} %q_hbm.1, bf16[4,128,128]{2,1,0:T(8,128)(2,1)} %bitcast.4, bf16[4,128,128]{2,1,0:T(8,128)(2,1)} %bitcast.5, bf16[512,128]{1,0:T(8,128)(2,1)} %w_hbm.1), custom_call_target="tpu_custom_call" | custom-call | tf_op jit(solution)/shard_map/pallas_call | solution.py:574
  84.3 1.9 %copy.8 = bf16[512,512]{1,0:T(8,128)(2,1)} copy(bf16[512,512]{1,0:T(8,128)(2,1)} %shard_map.64) | data formatting | bytes 1048576
